TPU v7x, 32 devices: a whole 2x2x4 slice. The times are simulated.
32 devices in a mesh: groups: 2 (over x), scen: 8 (over z, y), rf: 2 (over core).
Axes of the slice: x: 2, y: 2, z: 4, core: 2. Of those that a mesh axis runs over, the one named last changes fastest.
Arguments:
- paths: bfloat16 [1024, 16, 1024], P(('groups', 'scen'), None, 'rf'), parts along dimension 0, may hold values from -6 to 6
- sens: bfloat16 [128, 16384], P(('groups', 'rf')), parts along dimension 0, may hold values from -0.5 to 0.5
- block_of: int32 [128], P(('groups', 'rf')), parts along dimension 0, may hold values from 0 to 7
- netting_of: int32 [16384], P(('groups', 'rf')), parts along dimension 0, may hold values from 0 to 511
- date_index: int32 [16], replicated, may hold values from 0 to 63
- discount: float32 [64], replicated, may hold values from 0.5 to 1
- default_prob: float32 [1024, 64], P('groups'), parts along dimension 0, may hold values from 0.02 to 0.2
Outputs:
- sens_grad: float32 [128, 16384], P(('groups', 'rf'), 'scen'), parts along dimension 0
- path_grad: float32 [1024, 16, 1024], P(('groups', 'scen'), None, 'rf'), parts along dimension 0
- cva: float32 [2], P('groups'), parts along dimension 0
There are 2 independent parts, one for each index of `groups`. A program takes and returns all parts, laid end to end along the dimension named above; an argument that names none is the same for every part. Nothing has to cross between parts.
All inputs are finite; a program needn't handle non-finite values.
Results may differ from a plain program's by a relative error of at most 0.0047.
Values may be sent and summed in bfloat16 or wider, within the bound.
A program may use at most 64 MiB of HBM per device.

v0:
```python
import jax
import jax.numpy as jnp
from jax import lax
from jax.sharding import PartitionSpec as P


def on_device(paths, sens, block_of, netting_of, date_index, discount, default_prob):
    scen_local, dates, local_factors = paths.shape
    row_count = scen_local * dates
    set_count = default_prob.shape[0]
    set_ids = jnp.arange(set_count, dtype=jnp.int32)

    def member_table(group_sets):
        return (group_sets[:, None] == set_ids[None, :]).astype(jnp.bfloat16)

    gathered = lax.all_gather(paths, "rf", axis=2, tiled=True)
    factors = gathered.shape[2]
    path_rows = gathered.reshape(row_count, factors)
    block_count, block_width = sens.shape
    trade_width = netting_of.shape[0] // block_count
    factor_width = block_width // trade_width
    group_count = block_count // 4
    sens_groups = sens.reshape(group_count, 4, factor_width, trade_width)
    block_groups = block_of.reshape(group_count, 4)
    set_groups = netting_of.reshape(group_count, 4 * trade_width)

    def factor_slices(group_blocks):
        return [
            lax.dynamic_slice_in_dim(
                path_rows, group_blocks[member] * factor_width, factor_width, 1
            )
            for member in range(4)
        ]

    def forward(partial_value, inputs):
        group_sens, group_blocks, group_sets = inputs
        slices = factor_slices(group_blocks)
        values = jnp.concatenate(
            [
                jnp.dot(slices[member], group_sens[member], preferred_element_type=jnp.float32)
                for member in range(4)
            ],
            axis=1,
        ).astype(jnp.bfloat16)
        return (
            partial_value
            + jnp.dot(values, member_table(group_sets), preferred_element_type=jnp.float32),
            None,
        )

    partial_value, _ = lax.scan(
        forward,
        jnp.zeros((row_count, set_count), jnp.float32),
        (sens_groups, block_groups, set_groups),
    )
    weight = discount[date_index][:, None] * jnp.transpose(default_prob[:, date_index])
    scen_total = scen_local * lax.axis_size("scen")
    netted = lax.psum(partial_value, "rf").reshape(scen_local, dates, set_count)
    local_cva = jnp.sum(jax.nn.softplus(netted) * weight[None])
    cva = lax.psum(local_cva, "scen") / scen_total
    adjoint = (
        (jax.nn.sigmoid(netted) * weight[None]).astype(jnp.bfloat16).reshape(row_count, set_count)
    )

    def backward(grad_paths, inputs):
        group_sens, group_blocks, group_sets = inputs
        slices = factor_slices(group_blocks)
        value_adj = jnp.einsum(
            "rn,tn->rt", adjoint, member_table(group_sets), preferred_element_type=jnp.float32
        ).astype(jnp.bfloat16)
        sens_terms = []
        for member in range(4):
            member_adj = value_adj[:, member * trade_width : (member + 1) * trade_width]
            sens_terms.append(
                jnp.einsum(
                    "rf,rt->ft", slices[member], member_adj, preferred_element_type=jnp.float32
                ).reshape(factor_width * trade_width)
            )
            path_term = jnp.einsum(
                "rt,ft->rf", member_adj, group_sens[member], preferred_element_type=jnp.float32
            )
            start = group_blocks[member] * factor_width
            current = lax.dynamic_slice_in_dim(grad_paths, start, factor_width, 1)
            grad_paths = lax.dynamic_update_slice_in_dim(grad_paths, current + path_term, start, 1)
        return (grad_paths, jnp.stack(sens_terms))

    grad_paths, sens_terms = lax.scan(
        backward,
        jnp.zeros((row_count, factors), jnp.float32),
        (sens_groups, block_groups, set_groups),
    )
    sens_grad = lax.psum_scatter(
        sens_terms.reshape(block_count, block_width), "scen", scatter_dimension=1, tiled=True
    )
    path_grad = lax.psum_scatter(grad_paths, "rf", scatter_dimension=1, tiled=True).reshape(
        scen_local, dates, factors // lax.axis_size("rf")
    )
    return (sens_grad, path_grad, jnp.reshape(cva, (1,)))


def solution(mesh):
    in_specs = (
        P(("groups", "scen"), None, "rf"),
        P(("groups", "rf"), None),
        P(("groups", "rf")),
        P(("groups", "rf")),
        P(),
        P(),
        P("groups", None),
    )
    out_specs = (P(("groups", "rf"), "scen"), P(("groups", "scen"), None, "rf"), P("groups"))
    return jax.shard_map(
        on_device, mesh=mesh, in_specs=in_specs, out_specs=out_specs, check_vma=False
    )
```

profile of v0, /device:TPU:0, one launch (start us, length us, event | category | flops | bytes accessed | tf_op | source)
XLA Modules:
  0.0 305.0 jit_solution(5628222089264343871)
XLA Ops:
  9.5 1.5 copy.14
  11.0 11.9 %all-gather.2.cloned.1.call-done = bf16[64,16,1024]{2,1,0:T(8,128)(2,1)} async-done(((bf16[64,16,512]{2,1,0:T(8,128)(2,1)}), bf16[64,16,1024]{2,1,0:T(8,128)(2,1)}) %all-gather.2.cloned.1.call-update) | async-done | bytes 2097168 | tf_op jit(solution)/shard_map/all_gather | solution.py:16
  22.9 73.3 %while.25 = (s32[]{:T(128)}, f32[1024,512]{1,0:T(8,128)S(1)}, s32[8,4]{0,1:T(4,128)S(1)}, bf16[1024,1024]{1,0:T(8,128)(2,1)}, bf16[8,4,128,128]{3,2,1,0:T(8,128)...) while((s32[]{:T(128)}, f32[1024,512]{1,0:T(8,128)S(1)}, ...), condition=%wide.region_1.2_spmd.clone, body=%wide.region_0.1_spmd.clone.sunk | while | flops 677117952 | bytes 7477727 | solution.py:51
  40.0 1.2 select_add_fusion.2
  49.1 1.2 select_add_fusion.2
  67.5 1.2 select_add_fusion.2
  95.0 1.2 select_add_fusion.2
  96.2 1.3 copy-done.5
  99.0 21.1 %all-reduce.2.cloned.1.call-done = f32[1024,512]{1,0:T(8,128)} async-done(((f32[1024,512]{1,0:T(8,128)}), f32[1024,512]{1,0:T(8,128)}) %all-reduce.2.cloned.1.call-update) | async-done | bytes 2097168 | tf_op jit(solution)/shard_map/psum | solution.py:58
  120.1 4.8 %fusion.53 = (f32[]{:T(128)}, bf16[1024,512]{1,0:T(8,128)(2,1)}) fusion(f32[1024,512]{1,0:T(8,128)} %all-reduce.2.cloned.1.call-done, f32[16,512]{1,0:T(8,128)S(1)} %broadcast_multiply_fusion), kind=kLoop, calls=%fused_computation.81 | loop fusion | flops 6815743 | bytes 3178500 | tf_op jit(solution)/shard_map/reduce_sum | solution.py:59
  124.9 2.5 broadcast_in_dim.13
  127.4 83.2 %while.24 = (s32[]{:T(128)}, f32[1024,1024]{1,0:T(8,128)}, f32[8,4,16384]{2,1,0:T(4,128)}, s32[8,4]{0,1:T(4,128)S(1)}, s32[8,512]{1,0:T(8,128)S(1)}, /*index=5*/...) while((s32[]{:T(128)}, f32[1024,1024]{1,0:T(8,128)}, ...), condition=%wide.region_4.5_spmd.clone, body=%wide.region_3.4_spmd.clone.sunk | while | flops 806813696 | bytes 43915816 | solution.py:87
  130.6 2.1 fusion.101
  135.9 1.9 copy-done.3
  141.0 2.1 fusion.101
  146.3 1.9 copy-done.3
  151.4 2.1 fusion.101
  156.7 1.9 copy-done.3
  161.8 2.1 fusion.101
  167.1 1.9 copy-done.3
  172.2 2.1 fusion.101
  177.5 1.9 copy-done.3
  182.6 2.1 fusion.101
  187.9 1.9 copy-done.3
  193.0 2.1 fusion.101
  198.3 1.9 copy-done.3
  203.4 2.1 fusion.101
  208.7 1.9 copy-done.3
  210.6 3.0 reshape.103
  214.2 22.3 %psum.15 = f32[]{:T(128)} all-reduce(f32[]{:T(128)} %get-tuple-element.196), channel_id=1, replica_groups=mesh['groups'=2,'scen'=8,'rf'=2] {'scen'}, use_global_device_ids=true, to_apply=%region_8.9 | all-reduce | flops 1 | bytes 8 | tf_op jit(solution)/shard_map/psum | solution.py:60
  237.1 46.3 %reduce-scatter.3.cloned.1.call-done = f32[32,2048]{1,0:T(8,128)} async-done(((f32[32,16384]{1,0:T(8,128)}), f32[32,2048]{1,0:T(8,128)}) %reduce-scatter.3.cloned.1.call-update) | async-done | bytes 262160 | tf_op jit(solution)/shard_map/reduce_scatter | solution.py:92
  283.5 13.9 %reduce-scatter.5.cloned.1.call-done = f32[1024,512]{1,0:T(8,128)} async-done(((f32[1024,1024]{1,0:T(8,128)}), f32[1024,512]{1,0:T(8,128)}) %reduce-scatter.5.cloned.1.call-update) | async-done | bytes 2097168 | tf_op jit(solution)/shard_map/reduce_scatter | solution.py:95
  (207 shorter events, 81.9 us)
Async XLA Ops:
  7.2 91.1 %copy-start = (f32[512,64]{0,1:T(8,128)S(1)}, f32[512,64]{0,1:T(8,128)}, u32[]{:S(2)}) copy-start(f32[512,64]{0,1:T(8,128)} %param.17) | copy-start | bytes 393220
  7.2 15.7 %all-gather.2.cloned.1.call-start = ((), (), s32[]{:S(2)}) async-start(), calls=%async_computation.2 | async-start | bytes 3145728 | tf_op jit(solution)/shard_map/all_gather | solution.py:16
  7.9 112.2 %all-reduce.2.cloned.1.call-start = ((), (), s32[]{:S(2)}) async-start(), calls=%async_computation.3 | async-start | bytes 4194304 | tf_op jit(solution)/shard_map/psum | solution.py:58
  96.2 1.3 copy-start.5
  96.2 1.4 copy-start.6
  96.2 1.4 copy-start.1
  97.5 185.9 %reduce-scatter.3.cloned.1.call-start = ((), (), s32[]{:S(2)}) async-start(), calls=%async_computation.4 | async-start | bytes 2359296 | tf_op jit(solution)/shard_map/reduce_scatter | solution.py:92
  124.9 2.5 copy-start.4
  130.5 4.2 %copy-start.2 = (f32[1024,1024]{1,0:T(8,128)S(1)}, f32[1024,1024]{1,0:T(8,128)}, u32[]{:S(2)}) copy-start(f32[1024,1024]{1,0:T(8,128)} %get-tuple-element.355) | copy-start | bytes 12582916 | tf_op jit(solution)/shard_map/while
  135.9 1.9 copy-start.3
  140.9 4.2 %copy-start.2 = (f32[1024,1024]{1,0:T(8,128)S(1)}, f32[1024,1024]{1,0:T(8,128)}, u32[]{:S(2)}) copy-start(f32[1024,1024]{1,0:T(8,128)} %get-tuple-element.355) | copy-start | bytes 12582916 | tf_op jit(solution)/shard_map/while
  146.3 1.9 copy-start.3
  151.3 4.2 %copy-start.2 = (f32[1024,1024]{1,0:T(8,128)S(1)}, f32[1024,1024]{1,0:T(8,128)}, u32[]{:S(2)}) copy-start(f32[1024,1024]{1,0:T(8,128)} %get-tuple-element.355) | copy-start | bytes 12582916 | tf_op jit(solution)/shard_map/while
  156.7 1.9 copy-start.3
  161.8 4.2 %copy-start.2 = (f32[1024,1024]{1,0:T(8,128)S(1)}, f32[1024,1024]{1,0:T(8,128)}, u32[]{:S(2)}) copy-start(f32[1024,1024]{1,0:T(8,128)} %get-tuple-element.355) | copy-start | bytes 12582916 | tf_op jit(solution)/shard_map/while
  167.1 1.9 copy-start.3
  172.2 4.2 %copy-start.2 = (f32[1024,1024]{1,0:T(8,128)S(1)}, f32[1024,1024]{1,0:T(8,128)}, u32[]{:S(2)}) copy-start(f32[1024,1024]{1,0:T(8,128)} %get-tuple-element.355) | copy-start | bytes 12582916 | tf_op jit(solution)/shard_map/while
  177.5 1.9 copy-start.3
  182.6 4.2 %copy-start.2 = (f32[1024,1024]{1,0:T(8,128)S(1)}, f32[1024,1024]{1,0:T(8,128)}, u32[]{:S(2)}) copy-start(f32[1024,1024]{1,0:T(8,128)} %get-tuple-element.355) | copy-start | bytes 12582916 | tf_op jit(solution)/shard_map/while
  187.9 1.9 copy-start.3
  193.0 4.2 %copy-start.2 = (f32[1024,1024]{1,0:T(8,128)S(1)}, f32[1024,1024]{1,0:T(8,128)}, u32[]{:S(2)}) copy-start(f32[1024,1024]{1,0:T(8,128)} %get-tuple-element.355) | copy-start | bytes 12582916 | tf_op jit(solution)/shard_map/while
  198.3 1.9 copy-start.3
  203.4 4.2 %copy-start.2 = (f32[1024,1024]{1,0:T(8,128)S(1)}, f32[1024,1024]{1,0:T(8,128)}, u32[]{:S(2)}) copy-start(f32[1024,1024]{1,0:T(8,128)} %get-tuple-element.355) | copy-start | bytes 12582916 | tf_op jit(solution)/shard_map/while
  208.7 1.9 copy-start.3
  213.6 83.7 %reduce-scatter.5.cloned.1.call-start = ((), (), s32[]{:S(2)}) async-start(), calls=%async_computation.5 | async-start | bytes 6291456 | tf_op jit(solution)/shard_map/reduce_scatter | solution.py:95
Sparse Core Ops, SparseCore 0:
  9.6 13.2 all-gather.1
  97.6 22.3 all-reduce.1
  213.7 69.6 reduce-scatter.2
  286.3 10.9 reduce-scatter.4
where the time goes:
time: 307 us; the launch traced here: 305 us
  waiting for transfers between devices  94.4 us (31%)
  matrix products  81.1 us (26%)
  loops' own time  41.6 us (14%)
  local copies, waits for them, and re-layouts  37.2 us (12%)
  blocking collectives  22.3 us (7%)
  between operations  15.7 us (5%)
  other arithmetic  12.6 us (4%)
    reduce_scatter x1, waiting for transfers between devices, on_device(): lax.psum_scatter(sens_terms.reshape(block_count, block_width), 'scen', sc...  46.3 us
    dot_general x32, matrix products, forward(): jnp.dot(slices[member], group_sens[member], preferred_element_type=jnp.fl...  37.3 us
    psum x1, blocking collectives, on_device(): cva = lax.psum(local_cva, 'scen') / scen_total  22.3 us
    psum x1, waiting for transfers between devices, on_device(): netted = lax.psum(partial_value, 'rf').reshape(scen_local, dates, set_count)  21.1 us
    another operation x1, loops' own time, on_device(): lax.scan(forward, jnp.zeros((row_count, set_count), jnp.float32), (sens_g...  21.1 us
    another operation x1, loops' own time, on_device(): lax.scan(backward, jnp.zeros((row_count, factors), jnp.float32), (sens_gr...  20.5 us
    dot_general x8, matrix products, backward(): jnp.einsum('rn,tn->rt', adjoint, member_table(group_sets), preferred_elem...  17 us
    while x32, local copies, waits for them, and re-layouts  15.6 us
  transfers between devices with their start and end apart: 4, of which 4 were waited for; matrix products, arithmetic and copies ran while one was open for 1% of the time, Pallas kernels for 0%

commit v1 on v0

v1 whole, which is shorter than its diff:
```python
import functools

import jax
import jax.numpy as jnp
from jax import lax
from jax.experimental import pallas as pl
from jax.experimental.pallas import tpu as pltpu
from jax.sharding import PartitionSpec as P

MESH = pl.DeviceIdType.MESH
F32 = jnp.float32
BF16 = jnp.bfloat16
NT = (((1,), (1,)), ((), ()))
NN = (((1,), (0,)), ((), ()))
TN = (((0,), (0,)), ((), ()))
UNROLL = 8
ROWS = 256


def dot(a, b, dims):
    return lax.dot_general(a, b, dims, preferred_element_type=F32)


def kernel(
    peers,
    paths,
    sens,
    block_of,
    netting,
    dates,
    discount,
    prob,
    sens_out,
    path_out,
    cva_out,
    paths_in,
    sens_rows,
    chain,
    table_send,
    table_recv,
    table,
    table_in,
    adj,
    adj_in,
    grad_send,
    grad_recv,
    cva_parts,
    reduced,
    cva_pair,
    picked,
    pair_send,
    pair_recv,
    ring_send,
    ring_recv,
):
    rows, own_factors = paths.shape
    blocks, width = netting.shape
    factor_blocks, fb, half = table.shape
    own_blocks = factor_blocks // 2
    window = dates.shape[0]
    share = fb // peers
    scen = lax.axis_index("scen")
    core = lax.axis_index("rf")
    other = 1 - core

    barrier = pltpu.get_barrier_semaphore()
    pl.semaphore_signal(barrier, inc=1, device_id={"rf": other}, device_id_type=MESH)
    for step in range(1, peers):
        pl.semaphore_signal(
            barrier,
            inc=1,
            device_id={"scen": lax.rem(scen + step, peers)},
            device_id_type=MESH,
        )

    def pair_copy(src, dst, slot):
        return pltpu.make_async_remote_copy(
            src_ref=src,
            dst_ref=dst,
            send_sem=pair_send.at[slot],
            recv_sem=pair_recv.at[slot],
            device_id={"rf": other},
            device_id_type=MESH,
        )

    def ring_copy(src, dst, slot, step):
        return pltpu.make_async_remote_copy(
            src_ref=src,
            dst_ref=dst,
            send_sem=ring_send.at[slot, step],
            recv_sem=ring_recv.at[slot, step],
            device_id={"scen": lax.rem(scen + step, peers)},
            device_id_type=MESH,
        )

    def spread(at, _):
        for k in range(8):
            f = at * 8 + k
            sens_rows[pl.ds(f, blocks, stride=fb), :] = sens[
                :, pl.ds(pl.multiple_of(f * width, width), width)
            ].astype(F32)
        return 0

    lax.fori_loop(0, fb // 8, spread, 0)
    pl.semaphore_wait(barrier, peers)
    copy_paths = pair_copy(paths, paths_in, 0)
    copy_paths.start()

    chain[0] = jnp.zeros((fb, half), F32)
    set_ids = lax.broadcasted_iota(jnp.int32, (half, width), 0)

    def build(base):
        ids = set_ids + base * half

        def body(at, last):
            terms = []
            for k in range(UNROLL):
                b = at * UNROLL + k
                member = (ids == netting[pl.ds(b, 1), :]).astype(F32).astype(BF16)
                block = sens_rows[pl.ds(pl.multiple_of(b * fb, fb), fb), :].astype(BF16)
                terms.append(dot(block, member, NT))
            for k in range(UNROLL):
                b = at * UNROLL + k
                mine = block_of[b]
                before = jnp.int32(0)
                for i in range(factor_blocks):
                    before = jnp.where(mine == i, last[i], before)
                chain[b + 1] = terms[k] + chain[before]
                last = tuple(jnp.where(mine == i, b + 1, last[i]) for i in range(factor_blocks))
            return last

        return lax.fori_loop(
            0, blocks // UNROLL, body, tuple(jnp.int32(0) for _ in range(factor_blocks))
        )

    last = build(other)
    for i in range(factor_blocks):
        table_send[i] = chain[last[i]].astype(BF16)
    copy_table = pair_copy(table_send, table_recv, 1)
    copy_table.start()
    last = build(core)

    row_id = lax.broadcasted_iota(jnp.int32, (window, discount.shape[1]), 0)
    col_id = lax.broadcasted_iota(jnp.int32, (window, discount.shape[1]), 1)
    curve = jnp.zeros((window, discount.shape[1]), F32)
    for w in range(window):
        curve = jnp.where(
            (row_id == w) & (col_id == dates[w]),
            jnp.broadcast_to(discount[...], curve.shape),
            curve,
        )
    own_prob = prob[pl.ds(pl.multiple_of(core * half, half), half), :]
    weight = lax.dot_general(
        curve, own_prob, NT, precision=lax.Precision.HIGHEST, preferred_element_type=F32
    )

    copy_table.wait()
    for i in range(factor_blocks):
        table[i] = (chain[last[i]] + table_recv[i].astype(F32)).astype(BF16)
    copy_side = pair_copy(table.at[pl.ds(other * own_blocks, own_blocks)], table_in, 2)
    copy_side.start()
    copy_paths.wait()

    own_table = table[pl.ds(core * own_blocks, own_blocks)].reshape(own_factors, half)
    other_table = table[pl.ds(other * own_blocks, own_blocks)].reshape(own_factors, half)

    def price(at, total):
        here = pl.ds(pl.multiple_of(at * ROWS, ROWS), ROWS)
        net = dot(paths[here, :], own_table, NN) + dot(paths_in[here, :], other_table, NN)
        net = net.reshape(ROWS // window, window, half)
        tail = jnp.exp(-jnp.abs(net))
        bottom = 1.0 + tail
        soft = jnp.maximum(net, 0.0) + jnp.log1p(tail)
        sig = jnp.where(net >= 0.0, 1.0, tail) / bottom
        adj[here, :] = (sig * weight[None]).reshape(ROWS, half).astype(BF16)
        term = jnp.sum((soft * weight[None]).reshape(ROWS // 8, 8, half), axis=0)
        return total + term

    total = lax.fori_loop(0, rows // ROWS, price, jnp.zeros((8, half), F32))
    folded = total[:, :128]
    for k in range(1, half // 128):
        folded = folded + total[:, k * 128 : (k + 1) * 128]
    cva_parts[0] = folded
    copy_adj = pair_copy(adj, adj_in, 3)
    copy_adj.start()

    for side, which in ((paths, core), (paths_in, other)):
        for k in range(own_blocks):
            grad = dot(side[:, k * fb : (k + 1) * fb], adj[...], TN).astype(BF16)
            for s in range(peers):
                grad_send[s, which * own_blocks + k] = grad[s * share : (s + 1) * share]
    sends = []
    for step in range(1, peers):
        to = lax.rem(scen + step, peers)
        sends.append(ring_copy(grad_send.at[to], grad_recv.at[step], 0, step))
        sends.append(ring_copy(cva_parts.at[0], cva_parts.at[step], 1, step))
    for copy in sends:
        copy.start()

    copy_side.wait()
    copy_adj.wait()
    own_side = table[pl.ds(core * own_blocks, own_blocks)].reshape(own_factors, half)
    in_side = table_in[...].reshape(own_factors, half)

    def paths_back(at, _):
        here = pl.ds(pl.multiple_of(at * ROWS, ROWS), ROWS)
        path_out[here, :] = dot(adj[here, :], own_side, NT) + dot(adj_in[here, :], in_side, NT)
        return 0

    lax.fori_loop(0, rows // ROWS, paths_back, 0)

    for copy in sends:
        copy.wait()
    acc = grad_send[scen].astype(F32)
    for step in range(1, peers):
        acc = acc + grad_recv[step].astype(F32)
    reduced[0] = acc
    cva = cva_parts[scen]
    for source in range(1, peers):
        cva = cva + cva_parts[lax.rem(scen - source + peers, peers)]
    cva_pair[0] = cva
    copy_sum = pair_copy(reduced.at[0], reduced.at[1], 4)
    copy_cva = pair_copy(cva_pair.at[0], cva_pair.at[1], 5)
    copy_sum.start()
    copy_cva.start()
    copy_sum.wait()
    copy_cva.wait()
    cva_out[0, 0] = jnp.sum(cva_pair[0] + cva_pair[1]) * (window / (rows * peers))

    for b in range(blocks):
        ids = jnp.broadcast_to(netting[b : b + 1, :], (share, width))
        lane = ids % width
        part = ids // width
        mine = block_of[b]
        low = reduced[core, mine]
        high = reduced[other, mine]
        out = jnp.zeros((share, width), F32)
        for k in range(2 * half // width):
            source = low if k < half // width else high
            at = (k % (half // width)) * width
            got = jnp.take_along_axis(source[:, at : at + width], lane, axis=1)
            out = jnp.where(part == k, got, out)
        picked[b * share : (b + 1) * share, :] = out
    for i in range(share):
        sens_out[:, i * width : (i + 1) * width] = picked[pl.ds(i, blocks, stride=share), :]


def on_device(paths, sens, block_of, netting_of, date_index, discount, default_prob):
    scen_local, window, own_factors = paths.shape
    rows = scen_local * window
    peers = lax.axis_size("scen")
    blocks, block_width = sens.shape
    width = netting_of.shape[0] // blocks
    fb = block_width // width
    sets, points = default_prob.shape
    half = sets // 2
    factor_blocks = 2 * own_factors // fb
    own_blocks = factor_blocks // 2
    share = fb // peers
    vmem = pl.BlockSpec(memory_space=pltpu.VMEM)
    smem = pl.BlockSpec(memory_space=pltpu.SMEM)
    flops = 2 * rows * own_factors * half * 8
    sens_grad, path_grad, cva = pl.pallas_call(
        functools.partial(kernel, peers),
        out_shape=(
            jax.ShapeDtypeStruct((blocks, block_width // peers), F32),
            jax.ShapeDtypeStruct((rows, own_factors), F32),
            jax.ShapeDtypeStruct((1, 1), F32),
        ),
        in_specs=[vmem, vmem, smem, vmem, smem, vmem, vmem],
        out_specs=(vmem, vmem, smem),
        scratch_shapes=[
            pltpu.VMEM((rows, own_factors), BF16),
            pltpu.VMEM((blocks * fb, width), F32),
            pltpu.VMEM((blocks + 1, fb, half), F32),
            pltpu.VMEM((factor_blocks, fb, half), BF16),
            pltpu.VMEM((factor_blocks, fb, half), BF16),
            pltpu.VMEM((factor_blocks, fb, half), BF16),
            pltpu.VMEM((own_blocks, fb, half), BF16),
            pltpu.VMEM((rows, half), BF16),
            pltpu.VMEM((rows, half), BF16),
            pltpu.VMEM((peers, factor_blocks, share, half), BF16),
            pltpu.VMEM((peers, factor_blocks, share, half), BF16),
            pltpu.VMEM((peers, 8, 128), F32),
            pltpu.VMEM((2, factor_blocks, share, half), F32),
            pltpu.VMEM((2, 8, 128), F32),
            pltpu.VMEM((blocks * share, width), F32),
            pltpu.SemaphoreType.DMA((6,)),
            pltpu.SemaphoreType.DMA((6,)),
            pltpu.SemaphoreType.DMA((2, peers)),
            pltpu.SemaphoreType.DMA((2, peers)),
        ],
        compiler_params=pltpu.CompilerParams(
            collective_id=0, has_side_effects=True, vmem_limit_bytes=48 * 1024 * 1024
        ),
        cost_estimate=pl.CostEstimate(
            flops=flops, bytes_accessed=rows * own_factors * 8, transcendentals=rows * sets
        ),
    )(
        paths.reshape(rows, own_factors),
        sens,
        block_of,
        netting_of.reshape(blocks, width),
        date_index,
        discount.reshape(1, points),
        default_prob,
    )
    return (
        sens_grad,
        path_grad.reshape(scen_local, window, own_factors),
        cva.reshape(1),
    )


def solution(mesh):
    in_specs = (
        P(("groups", "scen"), None, "rf"),
        P(("groups", "rf"), None),
        P(("groups", "rf")),
        P(("groups", "rf")),
        P(),
        P(),
        P("groups", None),
    )
    out_specs = (P(("groups", "rf"), "scen"), P(("groups", "scen"), None, "rf"), P("groups"))
    return jax.shard_map(
        on_device, mesh=mesh, in_specs=in_specs, out_specs=out_specs, check_vma=False
    )
```

time: 307 us -> 37.5 us (0.12)
  the two profiles are of different devices: /device:TPU:0 before, /device:TPU:13 now
where the time goes in v1:
time: 37.5 us; the launch traced here: 37.2 us
  Pallas kernels  26.5 us (71%)
  local copies, waits for them, and re-layouts  8.18 us (22%)
  between operations  2.48 us (7%)
    pallas_call x1, Pallas kernels, on_device(): pl.pallas_call(functools.partial(kernel, peers), out_shape=(jax.ShapeDtyp...  26.5 us
    unnamed x15, local copies, waits for them, and re-layouts  8.18 us

profile of v1, /device:TPU:13, one launch (start us, length us, event | category | flops | bytes accessed | tf_op | source)
XLA Modules:
  0.0 37.2 jit_solution(9417275512573801977)
XLA Ops:
  0.6 1.0 %copy.10.prob = f32[512,64]{1,0:T(8,128)S(1)} copy(f32[512,64]{0,1:T(8,128)} %param.13) | data formatting | bytes 262144 | tf_op args[6]
  1.7 0.0 copy-start
  1.7 1.2 %copy-done = bf16[64,16,512]{2,1,0:T(8,128)(2,1)S(1)} copy-done((bf16[64,16,512]{2,1,0:T(8,128)(2,1)S(1)}, bf16[64,16,512]{2,1,0:T(8,128)(2,1)}, u32[]{:S(2)}) %copy-start) | copy-done | bytes 1048600
  2.9 0.0 copy-start.1
  2.9 1.2 %copy-done.1 = bf16[32,16384]{1,0:T(8,128)(2,1)S(1)} copy-done((bf16[32,16384]{1,0:T(8,128)(2,1)S(1)}, bf16[32,16384]{1,0:T(8,128)(2,1)}, u32[]{:S(2)}) %copy-start.1) | copy-done | bytes 1048600
  4.1 0.0 copy-start.2
  4.1 0.7 %copy-done.2 = s32[4096]{0:T(1024)S(1)} copy-done((s32[4096]{0:T(1024)S(1)}, s32[4096]{0:T(1024)}, u32[]{:S(2)}) %copy-start.2) | copy-done | bytes 16408
  4.8 0.0 copy-start.3
  4.8 0.7 %copy-done.3 = s32[32]{0:T(128)S(1)} copy-done((s32[32]{0:T(128)S(1)}, s32[32]{0:T(128)}, u32[]{:S(2)}) %copy-start.3) | copy-done | bytes 152
  5.5 0.0 copy-start.4
  5.5 0.7 %copy-done.4 = s32[16]{0:T(128)S(1)} copy-done((s32[16]{0:T(128)S(1)}, s32[16]{0:T(128)}, u32[]{:S(2)}) %copy-start.4) | copy-done | bytes 88
  6.1 0.0 copy-start.5
  6.2 0.7 %copy-done.5 = f32[64]{0:T(128)S(1)} copy-done((f32[64]{0:T(128)S(1)}, f32[64]{0:T(128)}, u32[]{:S(2)}) %copy-start.5) | copy-done | bytes 280
  6.8 26.5 %shard_map.94 = (f32[32,2048]{1,0:T(8,128)S(1)}, f32[1024,512]{1,0:T(8,128)S(1)}, f32[1,1]{1,0:T(1,128)}) custom-call(bf16[1024,512]{1,0:T(8,128)(2,1)S(1)} %bitcast.6, bf16[32,16384]{1,0:T(8,128)(2,1)S(1)} %copy-done.1, s32[32]{0:T(128)S(1)} %copy-done.3, s32[32,128]{1,0:T(8,128)S(1)} %bitcast.7, s32[16]{0:T(128)S(1)} %copy-done.4, f32[1,64]{1,0:T(1,128)S(1)} %bitcast.8, ...), custom_call_target="tpu_custom_call" | custom-call | flops 2147483648 | bytes 4194304 | tf_op jit(solution)/shard_map/pallas_call | solution.py:263
  33.3 0.7 %copy.14 = f32[32,2048]{1,0:T(8,128)} copy(f32[32,2048]{1,0:T(8,128)S(1)} %get-tuple-element.12) | data formatting | bytes 524288
  34.0 1.3 %copy.15 = f32[64,16,512]{2,1,0:T(8,128)} copy(f32[64,16,512]{2,1,0:T(8,128)S(1)} %bitcast.5) | data formatting | bytes 4194304
Async XLA Ops:
  1.7 1.2 %copy-start = (bf16[64,16,512]{2,1,0:T(8,128)(2,1)S(1)}, bf16[64,16,512]{2,1,0:T(8,128)(2,1)}, u32[]{:S(2)}) copy-start(bf16[64,16,512]{2,1,0:T(8,128)(2,1)} %param.7) | copy-start | bytes 3145732
  2.9 1.2 %copy-start.1 = (bf16[32,16384]{1,0:T(8,128)(2,1)S(1)}, bf16[32,16384]{1,0:T(8,128)(2,1)}, u32[]{:S(2)}) copy-start(bf16[32,16384]{1,0:T(8,128)(2,1)} %sens.1) | copy-start | bytes 3145732
  4.1 0.7 %copy-start.2 = (s32[4096]{0:T(1024)S(1)}, s32[4096]{0:T(1024)}, u32[]{:S(2)}) copy-start(s32[4096]{0:T(1024)} %param.10) | copy-start | bytes 49156
  4.8 0.7 %copy-start.3 = (s32[32]{0:T(128)S(1)}, s32[32]{0:T(128)}, u32[]{:S(2)}) copy-start(s32[32]{0:T(128)} %block_of.1) | copy-start | bytes 388
  5.5 0.7 %copy-start.4 = (s32[16]{0:T(128)S(1)}, s32[16]{0:T(128)}, u32[]{:S(2)}) copy-start(s32[16]{0:T(128)} %dates.1) | copy-start | bytes 196
  6.1 0.7 %copy-start.5 = (f32[64]{0:T(128)S(1)}, f32[64]{0:T(128)}, u32[]{:S(2)}) copy-start(f32[64]{0:T(128)} %param.12) | copy-start | bytes 772

commit v2 on v1

v2 whole, which is shorter than its diff:
```python
import functools

import jax
import jax.numpy as jnp
from jax import lax
from jax.experimental import pallas as pl
from jax.experimental.pallas import tpu as pltpu
from jax.sharding import PartitionSpec as P

MESH = pl.DeviceIdType.MESH
F32 = jnp.float32
BF16 = jnp.bfloat16
NT = (((1,), (1,)), ((), ()))
NN = (((1,), (0,)), ((), ()))
TN = (((0,), (0,)), ((), ()))
UNROLL = 8
ROWS = 256
PIECES = 4
STAGE = 99


def dot(a, b, dims):
    return lax.dot_general(a, b, dims, preferred_element_type=F32)


def kernel(
    outer,
    inner,
    paths_hbm,
    sens_hbm,
    block_hbm,
    netting_hbm,
    dates_hbm,
    discount_hbm,
    prob_hbm,
    sums_out,
    path_out,
    cva_out,
    paths,
    sens,
    block_of,
    netting,
    dates,
    discount,
    prob,
    paths_in,
    sens_rows,
    chain,
    table_send,
    table_recv,
    table,
    table_in,
    adj,
    adj_in,
    grad_send,
    grad_recv,
    half_send,
    half_recv,
    cva_near,
    cva_far,
    reduced,
    cva_pair,
    path_rows,
    path_sem,
    load_sem,
    pair_send,
    pair_recv,
    near_send,
    near_recv,
    far_send,
    far_recv,
):
    rows, own_factors = paths.shape
    blocks, width = netting.shape
    factor_blocks, fb, half = table.shape
    own_blocks = factor_blocks // 2
    window = dates.shape[0]
    peers = outer * inner
    share = fb // peers
    pieces = grad_send.shape[0]
    piece_blocks = factor_blocks // pieces
    scen = lax.axis_index("scen")
    row = lax.div(scen, inner)
    place = lax.rem(scen, inner)
    core = lax.axis_index("rf")
    other = 1 - core

    loads = [
        pltpu.make_async_copy(src, dst, load_sem.at[k])
        for k, (src, dst) in enumerate(
            (
                (sens_hbm, sens),
                (netting_hbm, netting),
                (block_hbm, block_of),
                (dates_hbm, dates),
                (discount_hbm, discount),
                (prob_hbm, prob),
                (paths_hbm, paths),
            )
        )
    ]
    for load in loads:
        load.start()
    def near(step):
        return row * inner + lax.rem(place + step, inner)

    def far(step):
        return lax.rem(row + step, outer) * inner + place

    barrier = pltpu.get_barrier_semaphore()
    pl.semaphore_signal(barrier, inc=1, device_id={"rf": other}, device_id_type=MESH)
    for step in range(1, inner):
        pl.semaphore_signal(barrier, inc=1, device_id={"scen": near(step)}, device_id_type=MESH)
    for step in range(1, outer):
        pl.semaphore_signal(barrier, inc=1, device_id={"scen": far(step)}, device_id_type=MESH)

    def pair_copy(src, dst, slot):
        return pltpu.make_async_remote_copy(
            src_ref=src,
            dst_ref=dst,
            send_sem=pair_send.at[slot],
            recv_sem=pair_recv.at[slot],
            device_id={"rf": other},
            device_id_type=MESH,
        )

    def near_copy(src, dst, slot, step):
        return pltpu.make_async_remote_copy(
            src_ref=src,
            dst_ref=dst,
            send_sem=near_send.at[slot, step],
            recv_sem=near_recv.at[slot, step],
            device_id={"scen": near(step)},
            device_id_type=MESH,
        )

    def far_copy(src, dst, slot, step):
        return pltpu.make_async_remote_copy(
            src_ref=src,
            dst_ref=dst,
            send_sem=far_send.at[slot, step],
            recv_sem=far_recv.at[slot, step],
            device_id={"scen": far(step)},
            device_id_type=MESH,
        )

    def spread(at, _):
        for k in range(8):
            f = at * 8 + k
            sens_rows[pl.ds(f, blocks, stride=fb), :] = sens[
                :, pl.ds(pl.multiple_of(f * width, width), width)
            ].astype(F32)
        return 0

    loads[0].wait()
    lax.fori_loop(0, fb // 8, spread, 0)
    for load in loads[1:]:
        load.wait()

    chain[0] = jnp.zeros((fb, half), F32)
    set_ids = lax.broadcasted_iota(jnp.int32, (half, width), 0)

    def build(base):
        ids = set_ids + base * half

        def body(at, last):
            terms = []
            for k in range(UNROLL):
                b = at * UNROLL + k
                member = (ids == netting[pl.ds(b, 1), :]).astype(F32).astype(BF16)
                block = sens_rows[pl.ds(pl.multiple_of(b * fb, fb), fb), :].astype(BF16)
                terms.append(dot(block, member, NT))
            for k in range(UNROLL):
                b = at * UNROLL + k
                mine = block_of[b]
                before = jnp.int32(0)
                for i in range(factor_blocks):
                    before = jnp.where(mine == i, last[i], before)
                chain[b + 1] = terms[k] + chain[before]
                last = tuple(jnp.where(mine == i, b + 1, last[i]) for i in range(factor_blocks))
            return last

        return lax.fori_loop(
            0, blocks // UNROLL, body, tuple(jnp.int32(0) for _ in range(factor_blocks))
        )

    last = build(other)
    for i in range(factor_blocks):
        table_send[i] = chain[last[i]]
    pl.semaphore_wait(barrier, outer + inner - 1)
    copy_table = pair_copy(table_send, table_recv, 1)
    copy_table.start()
    copy_paths = pair_copy(paths, paths_in, 0)
    copy_paths.start()
    last = build(core)

    row_id = lax.broadcasted_iota(jnp.int32, (window, discount.shape[1]), 0)
    col_id = lax.broadcasted_iota(jnp.int32, (window, discount.shape[1]), 1)
    curve = jnp.zeros((window, discount.shape[1]), F32)
    for w in range(window):
        curve = jnp.where(
            (row_id == w) & (col_id == dates[w]),
            jnp.broadcast_to(discount[...], curve.shape),
            curve,
        )
    own_prob = prob[:, pl.ds(pl.multiple_of(core * half, half), half)]
    weight = lax.dot_general(
        curve, own_prob, NN, precision=lax.Precision.HIGHEST, preferred_element_type=F32
    )

    copy_table.wait()
    for i in range(factor_blocks):
        table[i] = (chain[last[i]] + table_recv[i]).astype(BF16)
    copy_side = pair_copy(table.at[pl.ds(other * own_blocks, own_blocks)], table_in, 2)
    copy_side.start()
    copy_paths.wait()
    if STAGE == 3:
        copy_side.wait()
        return

    own_table = table[pl.ds(core * own_blocks, own_blocks)].reshape(own_factors, half)
    other_table = table[pl.ds(other * own_blocks, own_blocks)].reshape(own_factors, half)

    def price(at, total):
        here = pl.ds(pl.multiple_of(at * ROWS, ROWS), ROWS)
        net = dot(paths[here, :], own_table, NN) + dot(paths_in[here, :], other_table, NN)
        net = net.reshape(ROWS // window, window, half)
        tail = jnp.exp(-jnp.abs(net))
        bottom = 1.0 + tail
        soft = jnp.maximum(net, 0.0) + jnp.log1p(tail)
        sig = jnp.where(net >= 0.0, 1.0, tail) / bottom
        adj[here, :] = (sig * weight[None]).reshape(ROWS, half).astype(BF16)
        term = jnp.sum((soft * weight[None]).reshape(ROWS // 8, 8, half), axis=0)
        return total + term

    total = lax.fori_loop(0, rows // ROWS, price, jnp.zeros((8, half), F32))
    folded = total[:, :128]
    for k in range(1, half // 128):
        folded = folded + total[:, k * 128 : (k + 1) * 128]
    cva_near[0] = folded
    copy_adj = pair_copy(adj, adj_in, 3)
    copy_adj.start()
    if STAGE == 4:
        copy_side.wait()
        copy_adj.wait()
        return

    cva_copies = [
        near_copy(cva_near.at[0], cva_near.at[step], pieces, step) for step in range(1, inner)
    ]
    for copy in cva_copies:
        copy.start()
    near_copies = []
    for piece in range(pieces):
        side, which = (paths, core) if piece < pieces // 2 else (paths_in, other)
        for k in range(piece_blocks):
            at = (piece % (pieces // 2)) * piece_blocks + k
            grad = dot(side[:, at * fb : (at + 1) * fb], adj[...], TN).astype(BF16)
            for s in range(peers):
                grad_send[piece, s % inner, s // inner, k] = grad[s * share : (s + 1) * share]
        copies = []
        for step in range(1, inner):
            to = lax.rem(place + step, inner)
            copies.append(
                near_copy(grad_send.at[piece, to], grad_recv.at[piece, step], piece, step)
            )
        for copy in copies:
            copy.start()
        near_copies.append(copies)
    if STAGE == 5:
        copy_side.wait()
        copy_adj.wait()
        for copy in sum(near_copies, []) + cva_copies:
            copy.wait()
        return

    copy_side.wait()
    copy_adj.wait()
    own_side = table[pl.ds(core * own_blocks, own_blocks)].reshape(own_factors, half)
    in_side = table_in[...].reshape(own_factors, half)
    stores = []

    def paths_back(at):
        here = pl.ds(at * ROWS, ROWS)
        path_rows[here, :] = dot(adj[here, :], own_side, NT) + dot(adj_in[here, :], in_side, NT)
        store = pltpu.make_async_copy(path_rows.at[here], path_out.at[here], path_sem.at[at])
        store.start()
        stores.append(store)

    far_copies = []
    for piece in range(pieces):
        if piece < rows // ROWS:
            paths_back(piece)
        for copy in near_copies[piece]:
            copy.wait()
        acc = grad_send[piece, place].astype(F32)
        for step in range(1, inner):
            acc = acc + grad_recv[piece, step].astype(F32)
        half_send[piece] = acc.astype(BF16)
        for step in range(1, outer):
            to = lax.rem(row + step, outer)
            copy = far_copy(half_send.at[piece, to], half_recv.at[piece, step], piece, step)
            copy.start()
            far_copies.append(copy)
    for copy in cva_copies:
        copy.wait()
    cva = cva_near[place]
    for source in range(1, inner):
        cva = cva + cva_near[lax.rem(place - source + inner, inner)]
    cva_far[0] = cva
    for step in range(1, outer):
        copy = far_copy(cva_far.at[0], cva_far.at[step], pieces, step)
        copy.start()
        far_copies.append(copy)

    for at in range(pieces, rows // ROWS):
        paths_back(at)
    for copy in far_copies:
        copy.wait()
    for store in stores:
        store.wait()
    if STAGE == 6:
        return
    for piece in range(pieces):
        acc = half_send[piece, row].astype(F32)
        for step in range(1, outer):
            acc = acc + half_recv[piece, step].astype(F32)
        which = core if piece < pieces // 2 else other
        at = (piece % (pieces // 2)) * piece_blocks
        reduced[0, pl.ds(which * own_blocks + at, piece_blocks)] = acc
    cva = cva_far[row]
    for source in range(1, outer):
        cva = cva + cva_far[lax.rem(row - source + outer, outer)]
    cva_pair[0] = cva
    copy_sum = pair_copy(reduced.at[0], reduced.at[1], 4)
    copy_cva = pair_copy(cva_pair.at[0], cva_pair.at[1], 5)
    copy_sum.start()
    copy_cva.start()
    copy_sum.wait()
    copy_cva.wait()
    sums_out[:, :, pl.ds(pl.multiple_of(core * half, half), half)] = reduced[0]
    sums_out[:, :, pl.ds(pl.multiple_of(other * half, half), half)] = reduced[1]
    cva_out[0, 0] = jnp.sum(cva_pair[0] + cva_pair[1]) * (window / (rows * peers))

def finish(
    sums_hbm, block_hbm, netting_hbm, path_in, sens_out, path_out, sums, block_of, netting, picked, held, sem, held_sem
):
    blocks, width = netting.shape
    share, sets = sums.shape[1:]
    moves = [
        pltpu.make_async_copy(src, dst, sem.at[k])
        for k, (src, dst) in enumerate(
            (
                (sums_hbm, sums),
                (netting_hbm, netting),
                (block_hbm, block_of),
            )
        )
    ]
    for move in moves:
        move.start()
    parts = held_sem.shape[1]
    size = held.shape[0] // parts
    ins, outs = [], []
    for k in range(parts):
        here = pl.ds(k * size, size)
        ins.append(pltpu.make_async_copy(path_in.at[here], held.at[here], held_sem.at[0, k]))
        outs.append(pltpu.make_async_copy(held.at[here], path_out.at[here], held_sem.at[1, k]))
    for copy in ins:
        copy.start()
    for move in moves:
        move.wait()
    for k in range(parts):
        ins[k].wait()
        outs[k].start()
    for b in range(blocks):
        ids = jnp.broadcast_to(netting[b : b + 1, :], (share, width))
        lane = lax.rem(ids, width)
        part = lax.div(ids, width)
        mine = sums[block_of[b]]
        out = jnp.zeros((share, width), F32)
        for k in range(sets // width):
            got = jnp.take_along_axis(mine[:, k * width : (k + 1) * width], lane, axis=1)
            out = jnp.where(part == k, got, out)
        picked[b * share : (b + 1) * share, :] = out
    for i in range(share):
        sens_out[:, i * width : (i + 1) * width] = picked[pl.ds(i, blocks, stride=share), :]
    for copy in outs:
        copy.wait()


def on_device(paths, sens, block_of, netting_of, date_index, discount, default_prob):
    scen_local, window, own_factors = paths.shape
    rows = scen_local * window
    peers = lax.axis_size("scen")
    blocks, block_width = sens.shape
    width = netting_of.shape[0] // blocks
    fb = block_width // width
    sets, points = default_prob.shape
    half = sets // 2
    factor_blocks = 2 * own_factors // fb
    own_blocks = factor_blocks // 2
    share = fb // peers
    inner = 1 << ((peers.bit_length() - 1) // 2)
    outer = peers // inner
    pieces = PIECES
    piece_blocks = factor_blocks // pieces
    vmem = pl.BlockSpec(memory_space=pltpu.VMEM)
    smem = pl.BlockSpec(memory_space=pltpu.SMEM)
    hbm = pl.BlockSpec(memory_space=pltpu.HBM)
    flops = 2 * rows * own_factors * half * 8
    netting = netting_of.reshape(blocks, width)
    sums, path_grad, cva = pl.pallas_call(
        functools.partial(kernel, outer, inner),
        out_shape=(
            jax.ShapeDtypeStruct((factor_blocks, share, sets), F32),
            jax.ShapeDtypeStruct((rows, own_factors), F32),
            jax.ShapeDtypeStruct((1, 1), F32),
        ),
        in_specs=[hbm] * 7,
        out_specs=(vmem, hbm, smem),
        scratch_shapes=[
            pltpu.VMEM((rows, own_factors), BF16),
            pltpu.VMEM((blocks, block_width), BF16),
            pltpu.SMEM((blocks,), jnp.int32),
            pltpu.VMEM((blocks, width), jnp.int32),
            pltpu.SMEM((window,), jnp.int32),
            pltpu.VMEM((1, points), F32),
            pltpu.VMEM((points, sets), F32),
            pltpu.VMEM((rows, own_factors), BF16),
            pltpu.VMEM((blocks * fb, width), F32),
            pltpu.VMEM((blocks + 1, fb, half), F32),
            pltpu.VMEM((factor_blocks, fb, half), F32),
            pltpu.VMEM((factor_blocks, fb, half), F32),
            pltpu.VMEM((factor_blocks, fb, half), BF16),
            pltpu.VMEM((own_blocks, fb, half), BF16),
            pltpu.VMEM((rows, half), BF16),
            pltpu.VMEM((rows, half), BF16),
            pltpu.VMEM((pieces, inner, outer, piece_blocks, share, half), BF16),
            pltpu.VMEM((pieces, inner, outer, piece_blocks, share, half), BF16),
            pltpu.VMEM((pieces, outer, piece_blocks, share, half), BF16),
            pltpu.VMEM((pieces, outer, piece_blocks, share, half), BF16),
            pltpu.VMEM((inner, 8, 128), F32),
            pltpu.VMEM((outer, 8, 128), F32),
            pltpu.VMEM((2, factor_blocks, share, half), F32),
            pltpu.VMEM((2, 8, 128), F32),
            pltpu.VMEM((rows, own_factors), F32),
            pltpu.SemaphoreType.DMA((rows // ROWS,)),
            pltpu.SemaphoreType.DMA((7,)),
            pltpu.SemaphoreType.DMA((6,)),
            pltpu.SemaphoreType.DMA((6,)),
            pltpu.SemaphoreType.DMA((pieces + 1, inner)),
            pltpu.SemaphoreType.DMA((pieces + 1, inner)),
            pltpu.SemaphoreType.DMA((pieces + 1, outer)),
            pltpu.SemaphoreType.DMA((pieces + 1, outer)),
        ],
        compiler_params=pltpu.CompilerParams(
            collective_id=0, has_side_effects=True, vmem_limit_bytes=56 * 1024 * 1024
        ),
        cost_estimate=pl.CostEstimate(
            flops=flops, bytes_accessed=rows * own_factors * 8, transcendentals=rows * sets
        ),
    )(
        paths.reshape(rows, own_factors),
        sens,
        block_of,
        netting,
        date_index,
        discount.reshape(1, points),
        default_prob.T,
    )
    sens_grad, path_grad = pl.pallas_call(
        finish,
        out_shape=(
            jax.ShapeDtypeStruct((blocks, block_width // peers), F32),
            jax.ShapeDtypeStruct((rows, own_factors), F32),
        ),
        in_specs=[hbm] * 4,
        out_specs=(vmem, hbm),
        scratch_shapes=[
            pltpu.VMEM((factor_blocks, share, sets), F32),
            pltpu.SMEM((blocks,), jnp.int32),
            pltpu.VMEM((blocks, width), jnp.int32),
            pltpu.VMEM((blocks * share, width), F32),
            pltpu.VMEM((rows, own_factors), F32),
            pltpu.SemaphoreType.DMA((3,)),
            pltpu.SemaphoreType.DMA((2, 4)),
        ],
        compiler_params=pltpu.CompilerParams(vmem_limit_bytes=56 * 1024 * 1024),
    )(sums, block_of, netting, path_grad)
    return (
        sens_grad,
        path_grad.reshape(scen_local, window, own_factors),
        cva.reshape(1),
    )


def solution(mesh):
    in_specs = (
        P(("groups", "scen"), None, "rf"),
        P(("groups", "rf"), None),
        P(("groups", "rf")),
        P(("groups", "rf")),
        P(),
        P(),
        P("groups", None),
    )
    out_specs = (P(("groups", "rf"), "scen"), P(("groups", "scen"), None, "rf"), P("groups"))
    return jax.shard_map(
        on_device, mesh=mesh, in_specs=in_specs, out_specs=out_specs, check_vma=False
    )
```

time: 37.5 us -> 34.9 us (0.931)
  the two profiles are of different devices: /device:TPU:13 before, /device:TPU:0 now
where the time goes in v2:
time: 34.9 us; the launch traced here: 34.7 us
  Pallas kernels  32.2 us (92%)
  between operations  2.46 us (7%)
    pallas_call x1, Pallas kernels, on_device(): pl.pallas_call(functools.partial(kernel, outer, inner), out_shape=(jax.Sh...  28.9 us
    pallas_call x1, Pallas kernels, on_device(): pl.pallas_call(finish, out_shape=(jax.ShapeDtypeStruct((blocks, block_wid...  3.38 us

profile of v2, /device:TPU:0, one launch (start us, length us, event | category | flops | bytes accessed | tf_op | source)
XLA Modules:
  0.0 34.7 jit_solution(17230579429548728586)
XLA Ops:
  0.6 28.9 %shard_map.94 = (f32[8,16,512]{2,1,0:T(8,128)}, f32[1024,512]{1,0:T(8,128)}, f32[1,1]{1,0:T(1,128)}) custom-call(bf16[1024,512]{1,0:T(8,128)(2,1)} %bitcast.9, bf16[32,16384]{1,0:T(8,128)(2,1)} %sens_hbm.1, s32[32]{0:T(128)} %block_hbm.3, s32[32,128]{1,0:T(8,128)} %bitcast.6, s32[16]{0:T(128)} %dates_hbm.1, f32[1,64]{1,0:T(1,128)} %bitcast.11, ...), custom_call_target="tpu_custom_call" | custom-call | flops 2147483648 | bytes 4194304 | tf_op jit(solution)/shard_map/pallas_call | solution.py:413
  29.5 3.4 %shard_map.95 = (f32[32,2048]{1,0:T(8,128)}, f32[1024,512]{1,0:T(8,128)}) custom-call(f32[8,16,512]{2,1,0:T(8,128)} %get-tuple-element.8.sums_hbm, s32[32]{0:T(128)} %block_hbm.3, s32[32,128]{1,0:T(8,128)} %bitcast.7, f32[1024,512]{1,0:T(8,128)} %get-tuple-element.9.path_in), custom_call_target="tpu_custom_call" | custom-call | tf_op jit(solution)/shard_map/pallas_call | solution.py:472

commit v3 on v2

--- a/solution.py
+++ b/solution.py
@@ -13,10 +13,9 @@
 NT = (((1,), (1,)), ((), ()))
 NN = (((1,), (0,)), ((), ()))
 TN = (((0,), (0,)), ((), ()))
-UNROLL = 8
-ROWS = 256
+UNROLL = 16
+ROWS = 512
 PIECES = 4
-STAGE = 99
 
 
 def dot(a, b, dims):
@@ -44,6 +43,7 @@
     discount,
     prob,
     paths_in,
+    turned,
     sens_rows,
     chain,
     table_send,
@@ -152,6 +152,9 @@
             ].astype(F32)
         return 0
 
+    pl.semaphore_wait(barrier, outer + inner - 1)
+    copy_paths = pair_copy(paths_hbm, paths_in, 0)
+    copy_paths.start()
     loads[0].wait()
     lax.fori_loop(0, fb // 8, spread, 0)
     for load in loads[1:]:
@@ -187,11 +190,8 @@
     last = build(other)
     for i in range(factor_blocks):
         table_send[i] = chain[last[i]]
-    pl.semaphore_wait(barrier, outer + inner - 1)
     copy_table = pair_copy(table_send, table_recv, 1)
     copy_table.start()
-    copy_paths = pair_copy(paths, paths_in, 0)
-    copy_paths.start()
     last = build(core)
 
     row_id = lax.broadcasted_iota(jnp.int32, (window, discount.shape[1]), 0)
@@ -208,15 +208,14 @@
         curve, own_prob, NN, precision=lax.Precision.HIGHEST, preferred_element_type=F32
     )
 
+    turned[core] = jnp.transpose(paths[...])
+    copy_paths.wait()
+    turned[other] = jnp.transpose(paths_in[...])
     copy_table.wait()
     for i in range(factor_blocks):
         table[i] = (chain[last[i]] + table_recv[i]).astype(BF16)
     copy_side = pair_copy(table.at[pl.ds(other * own_blocks, own_blocks)], table_in, 2)
     copy_side.start()
-    copy_paths.wait()
-    if STAGE == 3:
-        copy_side.wait()
-        return
 
     own_table = table[pl.ds(core * own_blocks, own_blocks)].reshape(own_factors, half)
     other_table = table[pl.ds(other * own_blocks, own_blocks)].reshape(own_factors, half)
@@ -240,10 +239,6 @@
     cva_near[0] = folded
     copy_adj = pair_copy(adj, adj_in, 3)
     copy_adj.start()
-    if STAGE == 4:
-        copy_side.wait()
-        copy_adj.wait()
-        return
 
     cva_copies = [
         near_copy(cva_near.at[0], cva_near.at[step], pieces, step) for step in range(1, inner)
@@ -252,10 +247,10 @@
         copy.start()
     near_copies = []
     for piece in range(pieces):
-        side, which = (paths, core) if piece < pieces // 2 else (paths_in, other)
+        which = core if piece < pieces // 2 else other
         for k in range(piece_blocks):
             at = (piece % (pieces // 2)) * piece_blocks + k
-            grad = dot(side[:, at * fb : (at + 1) * fb], adj[...], TN).astype(BF16)
+            grad = dot(turned[which, at * fb : (at + 1) * fb, :], adj[...], NN).astype(BF16)
             for s in range(peers):
                 grad_send[piece, s % inner, s // inner, k] = grad[s * share : (s + 1) * share]
         copies = []
@@ -267,12 +262,6 @@
         for copy in copies:
             copy.start()
         near_copies.append(copies)
-    if STAGE == 5:
-        copy_side.wait()
-        copy_adj.wait()
-        for copy in sum(near_copies, []) + cva_copies:
-            copy.wait()
-        return
 
     copy_side.wait()
     copy_adj.wait()
@@ -319,8 +308,6 @@
         copy.wait()
     for store in stores:
         store.wait()
-    if STAGE == 6:
-        return
     for piece in range(pieces):
         acc = half_send[piece, row].astype(F32)
         for step in range(1, outer):
@@ -428,6 +415,7 @@
             pltpu.VMEM((1, points), F32),
             pltpu.VMEM((points, sets), F32),
             pltpu.VMEM((rows, own_factors), BF16),
+            pltpu.VMEM((2, own_factors, rows), BF16),
             pltpu.VMEM((blocks * fb, width), F32),
             pltpu.VMEM((blocks + 1, fb, half), F32),
             pltpu.VMEM((factor_blocks, fb, half), F32),

time: 34.9 us -> 32.9 us (0.943)
  Pallas kernels: 32.2 us -> 30.3 us
    pallas_call x1, Pallas kernels: 28.9 us -> 26.9 us  [on_device(): pl.pallas_call(functools.partial(kernel, outer, inner), out_shape=(jax.Sh...]
where the time goes in v3:
time: 32.9 us; the launch traced here: 32.7 us
  Pallas kernels  30.3 us (92%)
  between operations  2.46 us (7%)
    pallas_call x1, Pallas kernels, on_device(): pl.pallas_call(functools.partial(kernel, outer, inner), out_shape=(jax.Sh...  26.9 us
    pallas_call x1, Pallas kernels, on_device(): pl.pallas_call(finish, out_shape=(jax.ShapeDtypeStruct((blocks, block_wid...  3.38 us

profile of v3, /device:TPU:0, one launch (start us, length us, event | category | flops | bytes accessed | tf_op | source)
XLA Modules:
  0.0 32.7 jit_solution(11876203815943900025)
XLA Ops:
  0.6 26.9 %shard_map.94 = (f32[8,16,512]{2,1,0:T(8,128)}, f32[1024,512]{1,0:T(8,128)}, f32[1,1]{1,0:T(1,128)}) custom-call(bf16[1024,512]{1,0:T(8,128)(2,1)} %bitcast.9, bf16[32,16384]{1,0:T(8,128)(2,1)} %sens_hbm.1, s32[32]{0:T(128)} %block_hbm.3, s32[32,128]{1,0:T(8,128)} %bitcast.6, s32[16]{0:T(128)} %dates_hbm.1, f32[1,64]{1,0:T(1,128)} %bitcast.11, ...), custom_call_target="tpu_custom_call" | custom-call | flops 2147483648 | bytes 4194304 | tf_op jit(solution)/shard_map/pallas_call | solution.py:400
  27.5 3.4 %shard_map.95 = (f32[32,2048]{1,0:T(8,128)}, f32[1024,512]{1,0:T(8,128)}) custom-call(f32[8,16,512]{2,1,0:T(8,128)} %get-tuple-element.8.sums_hbm, s32[32]{0:T(128)} %block_hbm.3, s32[32,128]{1,0:T(8,128)} %bitcast.7, f32[1024,512]{1,0:T(8,128)} %get-tuple-element.9.path_in), custom_call_target="tpu_custom_call" | custom-call | tf_op jit(solution)/shard_map/pallas_call | solution.py:460

commit v4 on v3

--- a/solution.py
+++ b/solution.py
@@ -15,7 +15,7 @@
 TN = (((0,), (0,)), ((), ()))
 UNROLL = 16
 ROWS = 512
-PIECES = 4
+PIECES = 8
 
 
 def dot(a, b, dims):
@@ -188,10 +188,12 @@
         )
 
     last = build(other)
+    table_copies = []
     for i in range(factor_blocks):
         table_send[i] = chain[last[i]]
-    copy_table = pair_copy(table_send, table_recv, 1)
-    copy_table.start()
+        copy = pair_copy(table_send.at[i], table_recv.at[i], 6 + i)
+        copy.start()
+        table_copies.append(copy)
     last = build(core)
 
     row_id = lax.broadcasted_iota(jnp.int32, (window, discount.shape[1]), 0)
@@ -211,8 +213,8 @@
     turned[core] = jnp.transpose(paths[...])
     copy_paths.wait()
     turned[other] = jnp.transpose(paths_in[...])
-    copy_table.wait()
     for i in range(factor_blocks):
+        table_copies[i].wait()
         table[i] = (chain[last[i]] + table_recv[i]).astype(BF16)
     copy_side = pair_copy(table.at[pl.ds(other * own_blocks, own_blocks)], table_in, 2)
     copy_side.start()
@@ -435,8 +437,8 @@
             pltpu.VMEM((rows, own_factors), F32),
             pltpu.SemaphoreType.DMA((rows // ROWS,)),
             pltpu.SemaphoreType.DMA((7,)),
-            pltpu.SemaphoreType.DMA((6,)),
-            pltpu.SemaphoreType.DMA((6,)),
+            pltpu.SemaphoreType.DMA((6 + factor_blocks,)),
+            pltpu.SemaphoreType.DMA((6 + factor_blocks,)),
             pltpu.SemaphoreType.DMA((pieces + 1, inner)),
             pltpu.SemaphoreType.DMA((pieces + 1, inner)),
             pltpu.SemaphoreType.DMA((pieces + 1, outer)),

time: 32.9 us -> 32.8 us (level)
  no operation moved by 1% of the time
where the time goes in v4:
time: 32.8 us; the launch traced here: 32.7 us
  Pallas kernels  30.2 us (92%)
  between operations  2.46 us (8%)
    pallas_call x1, Pallas kernels, on_device(): pl.pallas_call(functools.partial(kernel, outer, inner), out_shape=(jax.Sh...  26.8 us
    pallas_call x1, Pallas kernels, on_device(): pl.pallas_call(finish, out_shape=(jax.ShapeDtypeStruct((blocks, block_wid...  3.38 us

profile of v4, /device:TPU:0, one launch (start us, length us, event | category | flops | bytes accessed | tf_op | source)
XLA Modules:
  0.0 32.7 jit_solution(14896467703341313895)
XLA Ops:
  0.6 26.8 %shard_map.94 = (f32[8,16,512]{2,1,0:T(8,128)}, f32[1024,512]{1,0:T(8,128)}, f32[1,1]{1,0:T(1,128)}) custom-call(bf16[1024,512]{1,0:T(8,128)(2,1)} %bitcast.9, bf16[32,16384]{1,0:T(8,128)(2,1)} %sens_hbm.1, s32[32]{0:T(128)} %block_hbm.3, s32[32,128]{1,0:T(8,128)} %bitcast.6, s32[16]{0:T(128)} %dates_hbm.1, f32[1,64]{1,0:T(1,128)} %bitcast.11, ...), custom_call_target="tpu_custom_call" | custom-call | flops 2147483648 | bytes 4194304 | tf_op jit(solution)/shard_map/pallas_call | solution.py:402
  27.5 3.4 %shard_map.95 = (f32[32,2048]{1,0:T(8,128)}, f32[1024,512]{1,0:T(8,128)}) custom-call(f32[8,16,512]{2,1,0:T(8,128)} %get-tuple-element.8.sums_hbm, s32[32]{0:T(128)} %block_hbm.3, s32[32,128]{1,0:T(8,128)} %bitcast.7, f32[1024,512]{1,0:T(8,128)} %get-tuple-element.9.path_in), custom_call_target="tpu_custom_call" | custom-call | tf_op jit(solution)/shard_map/pallas_call | solution.py:462
